TPU v7x, 32 devices: a whole 2x2x4 slice. The times are simulated.
32 devices in a mesh: groups: 2 (over y), occ: 4 (over z), aux: 4 (over x, core).
Axes of the slice: x: 2, y: 2, z: 4, core: 2. Of those that a mesh axis runs over, the one named last changes fastest.
Arguments:
- b_tensor: float32 [8, 2560, 1800], P(('groups', 'occ'), 'aux'), parts along dimension 0, may hold values from -2 to 2
- eps_occ: float32 [8], P(('groups', 'occ')), parts along dimension 0, may hold values from -2 to -0.3
- eps_virt: float32 [3600], P('groups'), parts along dimension 0, may hold values from 0.2 to 4
Outputs:
- gamma: float32 [8, 2560, 64], P(('groups', 'occ'), 'aux'), parts along dimension 0
- pair_energy: float32 [8, 2], P(('groups', 'occ')), parts along dimension 0
There are 2 independent parts, one for each index of `groups`. A program takes and returns all parts, laid end to end along the dimension named above; each array names one. Nothing has to cross between parts.
All inputs are finite; a program needn't handle non-finite values.
Results may differ from a plain program's by a relative error of at most 0.0003.
Values sent between devices are 32-bit elements; how exact they have to be, the bound alone decides.
A program may use at most 64 MiB of HBM per device.

v0:
```python
import jax
import jax.numpy as jnp
from jax import lax
from jax.sharding import PartitionSpec as P

VB = 64


def shifted(x, axis, by):
    length = lax.axis_size(axis)
    return lax.ppermute(x, axis, [(i, (i + by) % length) for i in range(length)])


def partial_products(own, other):
    hp = lax.Precision.HIGHEST
    coul = jnp.einsum("qa,qb->ab", own[:, :VB], other, precision=hp)
    exch = jnp.einsum("qa,qb->ab", other[:, :VB], own, precision=hp)
    return (coul, exch)


def body(b_tensor, eps_occ, eps_virt):
    hp = lax.Precision.HIGHEST
    own = b_tensor[0]
    e_own = eps_occ[0]
    total = jnp.zeros((own.shape[0], VB), jnp.float32)
    energies = []
    partners = []
    current = (b_tensor, eps_occ)
    for step in range(2):
        current = shifted((current[0], current[1]), "occ", 1)
        partners.append(current)
    for partner in partners:
        other = partner[0][0]
        e_other = partner[1][0]
        coul_part, exch_part = partial_products(own, other)
        coul, exch = lax.psum((coul_part, exch_part), "aux")
        denom = eps_virt[:VB, None] + eps_virt[None, :] - e_own - e_other
        amp = (2.0 * coul - exch) / denom
        energy = jnp.sum(coul * amp)
        energies.append(energy)
        total = total + jnp.einsum("qb,ab->qa", other, amp, precision=hp)
    return (total[None], jnp.stack(energies)[None])


def solution(mesh):
    placed = (P(("groups", "occ"), "aux", None), P(("groups", "occ")), P("groups"))
    return jax.shard_map(
        body,
        mesh=mesh,
        in_specs=placed,
        out_specs=(P(("groups", "occ"), "aux", None), P(("groups", "occ"), None)),
        check_vma=False,
    )
```

profile of v0, /device:TPU:0, one launch (start us, length us, event | category | flops | bytes accessed | tf_op | source)
XLA Modules:
  0.0 296.1 jit_solution(15913005922092299135)
XLA Ops:
  7.2 0.0 all-reduce.3.cloned.1.call-start
  7.2 0.0 copy-start
  7.2 3.1 %collective-permute-start = (f32[1,640,1800]{1,2,0:T(8,128)}, f32[1,640,1800]{1,2,0:T(8,128)S(1)}, u32[]{:S(2)}, u32[]{:S(2)}) collective-permute-start(f32[1,640,1800]{1,2,0:T(8,128)} %param.3), channel_id=1, source_target_pairs={{0,4},{4,8},{8,12},{12,0},{1,5},{5,9},{9,13},{13,1},{2,6},{6,10},{... | collective-permute-start | bytes 13824008 | tf_op jit(solution)/shard_map/ppermute | solution.py:11
  10.3 101.7 %collective-permute-done = f32[1,640,1800]{1,2,0:T(8,128)S(1)} collective-permute-done((f32[1,640,1800]{1,2,0:T(8,128)}, f32[1,640,1800]{1,2,0:T(8,128)S(1)}, u32[]{:S(2)}, u32[]{:S(2)}) %collective-permute-start) | collective-permute-done | bytes 4608032 | tf_op jit(solution)/shard_map/ppermute | solution.py:11
  112.0 0.0 copy-start.3
  112.0 0.0 collective-permute-start.2
  112.0 9.0 %fusion.3 = f32[64,1800]{1,0:T(8,128)} fusion(f32[640,1800]{0,1:T(8,128)S(1)} %bitcast.32, f32[1,640,1800]{1,2,0:T(8,128)} %param.3), kind=kOutput, calls=%fused_computation.9 | convolution fusion | flops 884736000 | bytes 5232640 | tf_op jit(solution)/shard_map/qa,qb->ab/dot_general | solution.py:17
  121.0 0.0 copy-done
  121.0 5.1 %fusion.7 = f32[64,1800]{1,0:T(8,128)} fusion(f32[640,1800]{0,1:T(8,128)S(1)} %bitcast.29, f32[1,640,1800]{1,2,0:T(8,128)S(1)} %collective-permute-done), kind=kOutput, calls=%fused_computation.13 | convolution fusion | flops 884736000 | bytes 5232640 | tf_op jit(solution)/shard_map/qa,qb->ab/dot_general | solution.py:16
  126.1 0.0 copy-done.3
  126.1 88.3 %collective-permute-done.2 = f32[1,640,1800]{1,2,0:T(8,128)S(1)} collective-permute-done((f32[1,640,1800]{1,2,0:T(8,128)S(1)}, f32[1,640,1800]{1,2,0:T(8,128)S(1)}, u32[]{:S(2)}, u32[]{:S(2)}) %collective-permute-start.2) | collective-permute-done | bytes 4608032 | tf_op jit(solution)/shard_map/ppermute | solution.py:11
  214.4 5.1 %fusion.1 = f32[64,1800]{1,0:T(8,128)} fusion(f32[640,1800]{0,1:T(8,128)S(1)} %bitcast.31, f32[1,640,1800]{1,2,0:T(8,128)S(1)} %copy-done), kind=kOutput, calls=%fused_computation.7 | convolution fusion | flops 884736000 | bytes 5232640 | tf_op jit(solution)/shard_map/qa,qb->ab/dot_general | solution.py:17
  219.5 0.0 copy-done.1
  219.6 0.0 copy-start.6
  219.6 5.3 %fusion.5 = f32[64,1800]{1,0:T(8,128)} fusion(f32[640,1800]{0,1:T(8,128)S(1)} %bitcast.30, f32[1,640,1800]{1,2,0:T(8,128)S(1)} %collective-permute-done.2), kind=kOutput, calls=%fused_computation.11 | convolution fusion | flops 884736000 | bytes 5232640 | tf_op jit(solution)/shard_map/qa,qb->ab/dot_general | solution.py:16
  224.9 0.0 all-reduce.3.cloned.1.call-update
  224.9 0.1 collective-permute-start.1
  225.7 0.0 copy-done.6
  225.7 4.7 %collective-permute-done.1 = f32[1]{0:T(128)} collective-permute-done((f32[1]{0:T(128)}, f32[1]{0:T(128)}, u32[]{:S(2)}, u32[]{:S(2)}) %collective-permute-start.1) | collective-permute-done | bytes 36 | tf_op jit(solution)/shard_map/ppermute | solution.py:11
  230.4 0.0 collective-permute-start.3
  230.4 5.3 %collective-permute-done.3 = f32[1]{0:T(128)} collective-permute-done((f32[1]{0:T(128)}, f32[1]{0:T(128)}, u32[]{:S(2)}, u32[]{:S(2)}) %collective-permute-start.3) | collective-permute-done | bytes 36 | tf_op jit(solution)/shard_map/ppermute | solution.py:11
  235.7 37.1 %all-reduce.3.cloned.1.call-done = (f32[64,1800]{1,0:T(8,128)}, f32[64,1800]{1,0:T(8,128)}, f32[64,1800]{1,0:T(8,128)}, f32[64,1800]{1,0:T(8,128)}) async-done(((f32[64,1800]{1,0:T(8,128)}, f32[64,1800]{1,0:T(8,128)}, f32[64,1800]{1,0:T(8,128)}, f32[64,1800]{1,0:T(8,128)}), (f32[64,1800]{1,0:T(8,128)}, f32[64,1800]{1,0:T(8,128)}, f32[64,1800]{1,0:T(8,128)}, ...) | async-done | bytes 1843216 | tf_op jit(solution)/shard_map/psum | solution.py:36
  272.9 0.0 copy-start.2
  272.9 0.0 copy-start.4
  272.9 0.0 copy-start.5
  272.9 4.3 %multiply_reduce_fusion.1 = (f32[]{:T(128)}, f32[]{:T(128)}) fusion(f32[64,1800]{1,0:T(8,128)} %get-tuple-element.5, f32[]{:T(128)} %bitcast.3, f32[]{:T(128)} %bitcast.28, f32[1800]{0:T(1024)S(1)} %copy-done.6, f32[64]{0:T(128)S(1)} %slice.16, f32[64,1800]{1,0:T(8,128)} %get-tuple-element.4, f32[64,1800]{1,0:T(8,128)} %get-tuple-element.7, f32[]{:T(128)} %bitcast.5, ...), kind=kLoop, calls=%fused_computation.3 | loop fusion | flops 1612798 | bytes 1850676 | tf_op jit(solution)/shard_map/reduce_sum | solution.py:39
  277.2 1.9 maximum_bitcast_fusion
  279.1 6.0 %fusion.11 = f32[64,640]{1,0:T(8,128)S(1)} fusion(f32[1,640,1800]{1,2,0:T(8,128)} %copy-done.3, f32[64,1800]{1,0:T(8,128)} %get-tuple-element.4, f32[64,1800]{1,0:T(8,128)} %get-tuple-element.5, f32[]{:T(128)} %bitcast.3, f32[]{:T(128)} %bitcast.26, f32[1800]{0:T(1024)S(1)} %copy-done.6, f32[64]{0:T(128)S(1)} %slice.16), kind=kOutput, calls=%fused_computation.18 | convolution fusion | flops 885427200 | bytes 5700904 | tf_op jit(solution)/shard_map/qb,ab->qa/dot_general | solution.py:41
  285.1 0.0 copy-done.2
  285.2 0.0 copy-done.4
  285.2 0.0 copy-done.5
  285.2 4.0 %fusion = f32[1,640,64]{1,2,0:T(8,128)} fusion(f32[64,640]{1,0:T(8,128)S(1)} %fusion.11, f32[1,640,1800]{1,2,0:T(8,128)S(1)} %copy-done.2, f32[64,1800]{1,0:T(8,128)S(1)} %copy-done.4, f32[64,1800]{1,0:T(8,128)S(1)} %copy-done.5, f32[]{:T(128)} %bitcast.5, f32[]{:T(128)} %bitcast.27, f32[1800]{0:T(1024)S(1)} %copy-done.6, f32[64]{0:T(128)S(1)} %slice.16), kind=kOutput, calls=%fused_computation.1 | convolution fusion | flops 885468160 | bytes 5864744 | tf_op jit(solution)/shard_map/qb,ab->qa/dot_general | solution.py:41
  (2 shorter events, 0.0 us)
Async XLA Ops:
  7.2 265.7 %all-reduce.3.cloned.1.call-start = ((), (), s32[]{:S(2)}) async-start(), calls=%async_computation | async-start | bytes 3932160 | tf_op jit(solution)/shard_map/psum | solution.py:36
  7.2 113.8 %copy-start = (f32[1,640,1800]{1,2,0:T(8,128)S(1)}, f32[1,640,1800]{1,2,0:T(8,128)}, u32[]{:S(2)}) copy-start(f32[1,640,1800]{1,2,0:T(8,128)} %param.3) | copy-start | bytes 13824004
  7.2 104.8 %collective-permute-start = (f32[1,640,1800]{1,2,0:T(8,128)}, f32[1,640,1800]{1,2,0:T(8,128)S(1)}, u32[]{:S(2)}, u32[]{:S(2)}) collective-permute-start(f32[1,640,1800]{1,2,0:T(8,128)} %param.3), channel_id=1, source_target_pairs={{0,4},{4,8},{8,12},{12,0},{1,5},{5,9},{9,13},{13,1},{2,6},{6,10},{... | collective-permute-start | bytes 13824008 | tf_op jit(solution)/shard_map/ppermute | solution.py:11
  112.0 14.2 %copy-start.3 = (f32[1,640,1800]{1,2,0:T(8,128)}, f32[1,640,1800]{1,2,0:T(8,128)S(1)}, u32[]{:S(2)}) copy-start(f32[1,640,1800]{1,2,0:T(8,128)S(1)} %collective-permute-done) | copy-start | bytes 13824004
  112.0 102.4 %collective-permute-start.2 = (f32[1,640,1800]{1,2,0:T(8,128)S(1)}, f32[1,640,1800]{1,2,0:T(8,128)S(1)}, u32[]{:S(2)}, u32[]{:S(2)}) collective-permute-start(f32[1,640,1800]{1,2,0:T(8,128)S(1)} %collective-permute-done), channel_id=1, source_target_pairs={{0,4},{4,8},{8,12},{12,0},{1,5},{5,9},{9,13},{13,1},{2,6},{6,10},{... | collective-permute-start | bytes 13824008 | tf_op jit(solution)/shard_map/ppermute | solution.py:11
  214.4 5.2 %copy-start.1 = (f32[1,640,1800]{1,2,0:T(8,128)}, f32[1,640,1800]{1,2,0:T(8,128)S(1)}, u32[]{:S(2)}) copy-start(f32[1,640,1800]{1,2,0:T(8,128)S(1)} %collective-permute-done.2) | copy-start | bytes 13824004
  219.6 6.1 %copy-start.6 = (f32[1800]{0:T(1024)S(1)}, f32[1800]{0:T(1024)}, u32[]{:S(2)}) copy-start(f32[1800]{0:T(1024)} %param.5) | copy-start | bytes 21604
  224.9 5.5 %collective-permute-start.1 = (f32[1]{0:T(128)}, f32[1]{0:T(128)}, u32[]{:S(2)}, u32[]{:S(2)}) collective-permute-start(f32[1]{0:T(128)} %param.4), channel_id=1, source_target_pairs={{0,4},{4,8},{8,12},{12,0},{1,5},{5,9},{9,13},{13,1},{2,6},{6,10},{... | collective-permute-start | bytes 20 | tf_op jit(solution)/shard_map/ppermute | solution.py:11
  230.4 5.3 %collective-permute-start.3 = (f32[1]{0:T(128)}, f32[1]{0:T(128)}, u32[]{:S(2)}, u32[]{:S(2)}) collective-permute-start(f32[1]{0:T(128)} %collective-permute-done.1), channel_id=1, source_target_pairs={{0,4},{4,8},{8,12},{12,0},{1,5},{5,9},{9,13},{13,1},{2,6},{6,10},{... | collective-permute-start | bytes 20 | tf_op jit(solution)/shard_map/ppermute | solution.py:11
  272.9 12.3 %copy-start.2 = (f32[1,640,1800]{1,2,0:T(8,128)S(1)}, f32[1,640,1800]{1,2,0:T(8,128)}, u32[]{:S(2)}) copy-start(f32[1,640,1800]{1,2,0:T(8,128)} %copy-done.1) | copy-start | bytes 13824004
  272.9 12.3 %copy-start.4 = (f32[64,1800]{1,0:T(8,128)S(1)}, f32[64,1800]{1,0:T(8,128)}, u32[]{:S(2)}) copy-start(f32[64,1800]{1,0:T(8,128)} %get-tuple-element.6) | copy-start | bytes 1382404
  272.9 12.3 %copy-start.5 = (f32[64,1800]{1,0:T(8,128)S(1)}, f32[64,1800]{1,0:T(8,128)}, u32[]{:S(2)}) copy-start(f32[64,1800]{1,0:T(8,128)} %get-tuple-element.7) | copy-start | bytes 1382404
Sparse Core Ops, SparseCore 0:
  225.0 47.7 all-reduce.2
where the time goes:
time: 296 us
  waiting for transfers between devices  237 us (80%)
  matrix products  34.7 us (12%)
  between operations  14.8 us (5%)
  other arithmetic  6.27 us (2%)
  starting transfers between devices  3.18 us (1%)
    ppermute x4, waiting for transfers between devices, shifted(): lax.ppermute(x, axis, [(i, (i + by) % length) for i in range(length)])  200 us
    psum x1, waiting for transfers between devices, body(): coul, exch = lax.psum((coul_part, exch_part), 'aux')  37.1 us
    dot_general x2, matrix products, partial_products(): exch = jnp.einsum('qa,qb->ab', other[:, :VB], own, precision=hp)  14.2 us
    dot_general x2, matrix products, partial_products(): coul = jnp.einsum('qa,qb->ab', own[:, :VB], other, precision=hp)  10.5 us
    dot_general x2, matrix products, body(): total = total + jnp.einsum('qb,ab->qa', other, amp, precision=hp)  10 us
  transfers between devices with their start and end apart: 5, of which 5 were waited for; matrix products, arithmetic and copies ran while one was open for 5% of the time, Pallas kernels for 0%

commit v1 on v0

v1 whole, which is shorter than its diff:
```python
import functools

import jax
import jax.numpy as jnp
from jax import lax
from jax.experimental import pallas as pl
from jax.experimental.pallas import tpu as pltpu
from jax.sharding import PartitionSpec as P

VB = 64
CHUNKS = 3
MESH = pl.DeviceIdType.MESH
F32 = jnp.float32
BF16 = jnp.bfloat16


def split(x):
    hi = x.astype(BF16)
    return hi, (x - hi.astype(F32)).astype(BF16)


def dot(x, y):
    return lax.dot_general(x, y, (((1,), (0,)), ((), ())), preferred_element_type=F32)


def dot_t(x, y):
    return lax.dot_general(x, y, (((1,), (1,)), ((), ())), preferred_element_type=F32)


def distinct(n):
    return sorted({1 % n, 2 % n, (n - 1) % n, (n - 2) % n} - {0})


def kernel(n, levels, chunks, nv, *refs):
    b_hbm, eo_ref, ev_ref, gout, eout = refs[:5]
    (first, bv, bhi, blo, st, srecv, a1, evp, evc, esend, eocc, amp, ex, eacc,
     gacc, gsend, grecv, psend, precv) = refs[5:24]
    cur = refs[24:25 + levels]
    rec = refs[25 + levels:25 + 2 * levels]
    load_sem, send_sem, recv_sem = refs[25 + 2 * levels:]

    offs = distinct(n)
    ne = len(offs)
    rows_all = ne * VB
    depth, width = bhi.shape
    w = width // chunks
    me = lax.axis_index("occ")
    aux = lax.axis_index("aux")
    bits = [lax.rem(lax.div(aux, 2 ** level), 2) for level in range(levels)]
    buddy = [aux + (1 - 2 * bits[level]) * 2 ** level for level in range(levels)]
    rows = VB >> levels

    starts = []
    lo = 0
    for level in range(levels):
        lo = lo + bits[level] * (VB >> (level + 1))
        starts.append(pl.multiple_of(lo, 8))
    lo = starts[-1]

    sends = []

    def occ_at(offset):
        return lax.rem(me + offset, n)

    def push(src, dst, target):
        k = len(sends)
        copy = pltpu.make_async_remote_copy(
            src_ref=src, dst_ref=dst, send_sem=send_sem.at[k], recv_sem=recv_sem.at[k],
            device_id=target, device_id_type=MESH)
        copy.start()
        sends.append(copy)
        return copy

    load_first = pltpu.make_async_copy(b_hbm.at[0, :, pl.ds(0, 128)], first, load_sem.at[0])
    load_first.start()
    load_all = pltpu.make_async_copy(b_hbm.at[0], bv, load_sem.at[1])
    load_all.start()

    barrier = pltpu.get_barrier_semaphore()
    for offset in offs:
        pl.semaphore_signal(barrier, inc=1, device_id={"occ": occ_at(offset)}, device_id_type=MESH)
    for level in range(levels):
        pl.semaphore_signal(barrier, inc=1, device_id={"aux": buddy[level]}, device_id_type=MESH)

    esend[...] = jnp.full((8, 128), eo_ref[0], F32)
    load_first.wait()
    st[...] = first[...].T[:VB]
    pl.semaphore_wait(barrier, ne + levels)

    s_copies = [push(st, srecv.at[k], {"occ": occ_at(n - offset)}) for k, offset in enumerate(offs)]
    e_copies = [push(esend, eocc.at[k - 1], {"occ": occ_at(n - k)}) for k in (1, 2)]

    evp[...] = jnp.ones_like(evp)
    evp[:, :nv] = ev_ref[...]
    evc[...] = jnp.broadcast_to(evp[:, :128], (128, 128)).T
    eacc[...] = jnp.zeros_like(eacc)
    bhi[:, width - 128:] = jnp.zeros((depth, 128), BF16)
    blo[:, width - 128:] = jnp.zeros((depth, 128), BF16)
    load_all.wait()

    @pl.loop(0, depth // 16)
    def _(t):
        block = pl.ds(pl.multiple_of(t * 16, 16), 16)
        hi, low = split(bv[block, :])
        bhi[block, :nv] = hi
        blo[block, :nv] = low

    for k in range(ne):
        s_copies[k].wait_recv()
        hi, low = split(srecv[k])
        a1[k * VB:(k + 1) * VB, :] = hi
        a1[rows_all + k * VB:rows_all + (k + 1) * VB, :] = low
    for copy in e_copies:
        copy.wait_recv()

    flying = {}

    def start_level(level, c):
        cols = pl.ds(c * w, w)
        half = VB >> (level + 1)
        away = pl.multiple_of((1 - bits[level]) * half, 8)
        flying["rs", level, c] = push(
            cur[level].at[:, pl.ds(away, half), cols], rec[level].at[:, :, cols], {"aux": buddy[level]})

    def start_gather(level, c):
        cols = pl.ds(c * w, w)
        block = amp.at[:, pl.ds(starts[level], VB >> (level + 1)), cols]
        flying["ag", level, c] = push(block, block, {"aux": buddy[level]})

    def products(c):
        cols = slice(c * w, (c + 1) * w)
        t = dot(a1[...], bhi[:, cols])
        u = dot(a1[:rows_all, :], blo[:, cols])
        cur[0][:, :, cols] = (t[:rows_all] + t[rows_all:] + u).reshape(ne, VB, w)
        start_level(0, c)

    def reduce_level(level, c):
        cols = slice(c * w, (c + 1) * w)
        half = VB >> (level + 1)
        flying["rs", level, c].wait_recv()
        keep = pl.multiple_of(bits[level] * half, 8)
        cur[level + 1][:, :, cols] = cur[level][:, pl.ds(keep, half), cols] + rec[level][:, :, cols]
        if level + 1 < levels:
            start_level(level + 1, c)
        else:
            for k in (1, 2):
                flying["ex", k, c] = push(
                    cur[levels].at[offs.index(n - k), :, pl.ds(c * w, w)],
                    ex.at[k - 1, :, pl.ds(c * w, w)], {"occ": occ_at(n - k)})

    def amplitudes(c):
        cols = slice(c * w, (c + 1) * w)
        for k in (1, 2):
            flying["ex", k, c].wait_recv()
            coul = cur[levels][offs.index(k), :, cols]
            exch = ex[k - 1, :, cols]
            base = evc[pl.ds(lo, rows), 0:1] - eocc[k - 1, 0:1, 0:1] - esend[0:1, 0:1]
            val = (2.0 * coul - exch) / (base + evp[:, cols])
            prod = coul * val
            part = eacc[k - 1]
            for t in range(w // 128):
                part = part + prod[:, t * 128:(t + 1) * 128]
            eacc[k - 1] = part
            if c == chunks - 1:
                column = lax.broadcasted_iota(jnp.int32, (rows, w), 1) + c * w
                val = jnp.where(column < nv, val, jnp.sum(part, axis=1, keepdims=True))
            amp[k - 1, pl.ds(lo, rows), cols] = val
        start_gather(levels - 1, c)

    def gather_level(level, c):
        flying["ag", level, c].wait_recv()
        start_gather(level - 1, c)

    final = []

    def gammas(c):
        cols = slice(c * w, (c + 1) * w)
        flying["ag", 0, c].wait_recv()
        if c == chunks - 1:
            for k in (1, 2):
                total = jnp.sum(amp[k - 1, :, width - 128:], axis=0, keepdims=True)
                psend[k - 1] = jnp.broadcast_to(total[:, 127:128], (8, 128))
                final.append(push(psend.at[k - 1], precv.at[k - 1], {"occ": occ_at(k)}))
        hi, low = split(amp[:, :, cols].reshape(2 * VB, w))
        t = dot_t(bhi[:, cols], jnp.concatenate([hi, low], axis=0))
        u = dot_t(blo[:, cols], hi)
        part = t[:, :2 * VB] + t[:, 2 * VB:] + u
        gacc[...] = part if c == 0 else gacc[...] + part

    stages = [products]
    stages += [functools.partial(reduce_level, level) for level in range(levels)]
    stages += [amplitudes]
    stages += [functools.partial(gather_level, level) for level in range(levels - 1, 0, -1)]
    stages += [gammas]
    for t in range(chunks + len(stages) - 1):
        for s, stage in enumerate(stages):
            if 0 <= t - s < chunks:
                stage(t - s)

    gsend[...] = gacc[...].T.reshape(2, VB, depth)
    g_copies = [push(gsend.at[k - 1], grecv.at[k - 1], {"occ": occ_at(k)}) for k in (1, 2)]
    for copy in final:
        copy.wait_recv()
    lane = lax.broadcasted_iota(jnp.int32, (8, 128), 1)
    eout[...] = jnp.where(lane == 0, precv[0], precv[1])[0:1, 0:2]
    for copy in g_copies:
        copy.wait_recv()
    gout[...] = grecv[0] + grecv[1]
    for copy in sends:
        copy.wait_send()


def body(n, m, b_tensor, eps_occ, eps_virt):
    _, depth, nv = b_tensor.shape
    width = (nv // 128 + 1) * 128
    levels = m.bit_length() - 1
    ne = len(distinct(n))
    tiles = width // 128
    chunks = CHUNKS if tiles % CHUNKS == 0 else 1
    rows = VB >> levels
    scratch = [
        pltpu.VMEM((depth, 128), F32),
        pltpu.VMEM((depth, nv), F32),
        pltpu.VMEM((depth, width), BF16),
        pltpu.VMEM((depth, width), BF16),
        pltpu.VMEM((VB, depth), F32),
        pltpu.VMEM((ne, VB, depth), F32),
        pltpu.VMEM((2 * ne * VB, depth), BF16),
        pltpu.VMEM((1, width), F32),
        pltpu.VMEM((128, 128), F32),
        pltpu.VMEM((8, 128), F32),
        pltpu.VMEM((2, 8, 128), F32),
        pltpu.VMEM((2, VB, width), F32),
        pltpu.VMEM((2, rows, width), F32),
        pltpu.VMEM((2, rows, 128), F32),
        pltpu.VMEM((depth, 2 * VB), F32),
        pltpu.VMEM((2, VB, depth), F32),
        pltpu.VMEM((2, VB, depth), F32),
        pltpu.VMEM((2, 8, 128), F32),
        pltpu.VMEM((2, 8, 128), F32),
    ]
    scratch += [pltpu.VMEM((ne, VB >> level, width), F32) for level in range(levels + 1)]
    scratch += [pltpu.VMEM((ne, VB >> (level + 1), width), F32) for level in range(levels)]
    copies = ne + 2 + chunks * (2 * levels + 2) + 4
    scratch += [
        pltpu.SemaphoreType.DMA((2,)),
        pltpu.SemaphoreType.DMA((copies,)),
        pltpu.SemaphoreType.DMA((copies,)),
    ]
    flops = 6 * depth * width * VB * (ne + 2)
    gamma, energy = pl.pallas_call(
        functools.partial(kernel, n, levels, chunks, nv),
        out_shape=(jax.ShapeDtypeStruct((VB, depth), F32), jax.ShapeDtypeStruct((1, 2), F32)),
        in_specs=[
            pl.BlockSpec(memory_space=pl.ANY),
            pl.BlockSpec(memory_space=pltpu.SMEM),
            pl.BlockSpec(memory_space=pltpu.VMEM),
        ],
        out_specs=(pl.BlockSpec(memory_space=pltpu.VMEM), pl.BlockSpec(memory_space=pltpu.VMEM)),
        scratch_shapes=scratch,
        compiler_params=pltpu.CompilerParams(
            collective_id=0, has_side_effects=True, vmem_limit_bytes=48 * 2 ** 20),
        cost_estimate=pl.CostEstimate(flops=flops, bytes_accessed=4 * depth * nv, transcendentals=0),
    )(b_tensor, eps_occ, eps_virt.reshape(1, nv))
    return gamma.T[None], energy


def solution(mesh):
    placed = (P(("groups", "occ"), "aux", None), P(("groups", "occ")), P("groups"))
    return jax.shard_map(
        functools.partial(body, mesh.shape["occ"], mesh.shape["aux"]),
        mesh=mesh,
        in_specs=placed,
        out_specs=(P(("groups", "occ"), "aux", None), P(("groups", "occ"), None)),
        check_vma=False,
    )
```

time: 296 us -> 68.1 us (0.23)
  waiting for transfers between devices: 237 us -> 0 us
  Pallas kernels: 0 us -> 56.5 us
  matrix products: 34.7 us -> 0 us
  between operations: 14.8 us -> 1.29 us
  local copies, waits for them, and re-layouts: 0.03 us -> 10.1 us
  other arithmetic: 6.27 us -> 0 us
  starting transfers between devices: 3.18 us -> 0 us
    ppermute x4 -> x0, waiting for transfers between devices: 200 us -> none  [shifted(): lax.ppermute(x, axis, [(i, (i + by) % length) for i in range(length)])]
    pallas_call x0 -> x1, Pallas kernels: none -> 56.5 us  [body(): pl.pallas_call(functools.partial(kernel, n, levels, chunks, nv), out_shap...]
    psum x1 -> x0, waiting for transfers between devices: 37.1 us -> none  [body(): coul, exch = lax.psum((coul_part, exch_part), 'aux')]
    dot_general x6 -> x0, matrix products: 34.7 us -> none  [the longest x2 14.2 us: partial_products(): exch = jnp.einsum('qa,qb->ab', other[:, :VB], own, precision=hp)]
    unnamed x14 -> x5, local copies, waits for them, and re-layouts: 0.03 us -> 9.39 us
    reduce_sum x1 -> x0, other arithmetic: 4.34 us -> none  [body(): energy = jnp.sum(coul * amp)]
    ppermute x4 -> x0, starting transfers between devices: 3.14 us -> none  [shifted(): lax.ppermute(x, axis, [(i, (i + by) % length) for i in range(length)])]
  transfers between devices with their start and end apart: 5 -> 0, of which waited for: 5 -> 0; matrix products, arithmetic and copies ran while one was open for 5% -> 0% of each run, Pallas kernels for 0% -> 0%
where the time goes in v1:
time: 68.1 us; the launch traced here: 67.9 us
  Pallas kernels  56.5 us (83%)
  local copies, waits for them, and re-layouts  10.1 us (15%)
  between operations  1.29 us (2%)
    pallas_call x1, Pallas kernels, body(): pl.pallas_call(functools.partial(kernel, n, levels, chunks, nv), out_shap...  56.5 us
    unnamed x5, local copies, waits for them, and re-layouts  9.39 us

profile of v1, /device:TPU:0, one launch (start us, length us, event | category | flops | bytes accessed | tf_op | source)
XLA Modules:
  0.0 67.9 jit_solution(1623606295694842844)
XLA Ops:
  1.3 0.7 %reshape.7.refs_2_ = f32[1,1800]{1,0:T(1,128)S(1)} reshape(f32[1800]{0:T(1024)} %param.5) | data formatting | bytes 14400 | tf_op jit(solution)/shard_map/reshape | solution.py:264
  2.0 5.8 %copy.5.refs_0_ = f32[1,640,1800]{2,1,0:T(8,128)} copy(f32[1,640,1800]{1,2,0:T(8,128)} %param.3) | data formatting | bytes 9216000 | tf_op args[0]
  7.8 0.0 copy-start
  7.8 2.4 %copy-done = f32[1,640,1800]{2,1,0:T(8,128)S(1)} copy-done((f32[1,640,1800]{2,1,0:T(8,128)S(1)}, f32[1,640,1800]{2,1,0:T(8,128)}, u32[]{:S(2)}) %copy-start) | copy-done | bytes 4608024
  10.2 56.5 %shard_map.50 = (f32[64,640]{1,0:T(8,128)S(1)}, f32[1,2]{1,0:T(1,128)S(1)}) custom-call(f32[1,640,1800]{2,1,0:T(8,128)S(1)} %copy-done, f32[1]{0:T(128)S(6)} %copy.8.refs_1_, f32[1,1800]{1,0:T(1,128)S(1)} %reshape.7.refs_2_), custom_call_target="tpu_custom_call" | custom-call | flops 2359296000 | bytes 4608000 | tf_op jit(solution)/shard_map/pallas_call | solution.py:251
  66.7 0.7 copy.9
  67.3 0.5 copy.10
Async XLA Ops:
  7.8 2.4 %copy-start = (f32[1,640,1800]{2,1,0:T(8,128)S(1)}, f32[1,640,1800]{2,1,0:T(8,128)}, u32[]{:S(2)}) copy-start(f32[1,640,1800]{2,1,0:T(8,128)} %copy.5.refs_0_) | copy-start | bytes 13824004

commit v2 on v1

v2 whole, which is shorter than its diff:
```python
import functools

import jax
import jax.numpy as jnp
from jax import lax
from jax.experimental import pallas as pl
from jax.experimental.pallas import tpu as pltpu
from jax.sharding import PartitionSpec as P

VB = 64
PARTS = {1: 3, 2: 1}
VMEM_MIB = 60
MESH = pl.DeviceIdType.MESH
F32 = jnp.float32
BF16 = jnp.bfloat16


def split(x):
    hi = x.astype(BF16)
    return hi, (x - hi.astype(F32)).astype(BF16)


def dot(x, y):
    return lax.dot_general(x, y, (((1,), (0,)), ((), ())), preferred_element_type=F32)


def dot_t(x, y):
    return lax.dot_general(x, y, (((1,), (1,)), ((), ())), preferred_element_type=F32)


def near(n, k):
    return sorted({k % n, (n - k) % n})


def schedule(levels, parts):
    first = [(2, c) for c in range(parts[2])]
    later = [(1, c) for c in range(parts[1])]
    order = [("products", 0, piece) for piece in first]
    for level in range(levels):
        order += [("reduce", level, piece) for piece in first]
    stages = [("products", 0)] + [("reduce", level) for level in range(levels)] + [("amplitudes", 0)]
    stages += [("gather", level) for level in range(levels - 1, 0, -1)] + [("gammas", 0)]
    rest = [("amplitudes", 0)] + [("gather", level) for level in range(levels - 1, 0, -1)] + [("gammas", 0)]
    for t in range(len(later) + len(stages) - 1):
        for s, stage in enumerate(stages):
            if 0 <= t - s < len(later):
                order.append((*stage, later[t - s]))
        if t >= 1 and rest:
            stage = rest.pop(0)
            order += [(*stage, piece) for piece in first]
    for stage in rest:
        order += [(*stage, piece) for piece in first]
    return order


def kernel(n, levels, parts, nv, *refs):
    b_hbm, eo_ref, ev_ref, gout, eout = refs[:5]
    (bv, bhi, blo, srecv, ahi, evp, evc, esend, eocc, amp, ex, eacc,
     gsend, grecv, psend, precv) = refs[5:21]
    at = 21
    cur, rec = {}, {}
    for k in (1, 2):
        cur[k] = refs[at:at + levels + 1]
        rec[k] = refs[at + levels + 1:at + 2 * levels + 1]
        at += 2 * levels + 1
    load_sem, send_sem, recv_sem = refs[at:]

    offs = sorted(set(near(n, 1) + near(n, 2)))
    ne = len(offs)
    width, depth = bhi.shape
    me = lax.axis_index("occ")
    aux = lax.axis_index("aux")
    bits = [lax.rem(lax.div(aux, 2 ** level), 2) for level in range(levels)]
    buddy = [aux + (1 - 2 * bits[level]) * 2 ** level for level in range(levels)]
    rows = VB >> levels

    starts = []
    lo = 0
    for level in range(levels):
        lo = lo + bits[level] * (VB >> (level + 1))
        starts.append(pl.multiple_of(lo, 8))
    lo = starts[-1]

    sends = []

    def occ_at(offset):
        return lax.rem(me + offset, n)

    def push(src, dst, target, slot=None, when=None):
        k = len(sends)
        copy = pltpu.make_async_remote_copy(
            src_ref=src, dst_ref=dst, send_sem=send_sem.at[k],
            recv_sem=recv_sem.at[ne + k if slot is None else slot],
            device_id=target, device_id_type=MESH)
        if when is None:
            copy.start()
        else:
            pl.when(when)(copy.start)
        sends.append((copy, when))
        return copy

    barrier = pltpu.get_barrier_semaphore()
    for offset in offs:
        pl.semaphore_signal(barrier, inc=1, device_id={"occ": occ_at(offset)}, device_id_type=MESH)
    for level in range(levels):
        pl.semaphore_signal(barrier, inc=1, device_id={"aux": buddy[level]}, device_id_type=MESH)
    load = pltpu.make_async_copy(b_hbm.at[0], bv.at[pl.ds(0, nv), :], load_sem.at[0])
    load.start()
    esend[...] = jnp.full((8, 128), eo_ref[0], F32)
    pl.semaphore_wait(barrier, ne + levels)

    batch = b_hbm.at[0, pl.ds(0, VB), :]
    arrivals = {}

    def share(offset, when=None):
        slot = offs.index(offset)
        arrivals[offset] = push(batch, srecv.at[slot], {"occ": occ_at(n - offset)}, slot, when)

    for offset in near(n, 2):
        share(offset)
    e_copies = [push(esend, eocc.at[k - 1], {"occ": occ_at(n - k)}) for k in (2, 1)]
    if n == 4:
        share(1, me > 0)
        share(3, me < 3)
    else:
        for offset in near(n, 1):
            share(offset)

    evp[...] = jnp.ones_like(evp)
    evp[:, :nv] = ev_ref[...]
    evc[...] = jnp.broadcast_to(evp[:, :128], (128, 128)).T
    eacc[...] = jnp.zeros_like(eacc)
    bv[nv:, :] = jnp.zeros((width - nv, depth), F32)
    load.wait()

    @pl.loop(0, width // 16)
    def _(t):
        block = pl.ds(pl.multiple_of(t * 16, 16), 16)
        hi, low = split(bv[block, :])
        bhi[block, :] = hi
        blo[block, :] = low

    if n == 4:
        arrivals[2].wait_recv()
        passed = srecv.at[offs.index(2)]
        push(passed, srecv.at[offs.index(1)], {"occ": occ_at(1)}, offs.index(1), me == 2)
        push(passed, srecv.at[offs.index(3)], {"occ": occ_at(3)}, offs.index(3), me == 1)

    flying = {}

    def span(piece):
        k, c = piece
        w = width // parts[k]
        return slice(c * w, (c + 1) * w), pl.ds(c * w, w), w

    def start_level(level, piece):
        k, c = piece
        _, cols, _ = span(piece)
        half = VB >> (level + 1)
        away = pl.multiple_of((1 - bits[level]) * half, 8)
        flying["reduce", level, piece] = push(
            cur[k][level].at[:, pl.ds(away, half), cols], rec[k][level].at[:, :, cols],
            {"aux": buddy[level]})

    def start_gather(level, piece):
        k, c = piece
        _, cols, _ = span(piece)
        block = amp.at[k - 1, pl.ds(starts[level], VB >> (level + 1)), cols]
        flying["gather", level, piece] = push(block, block, {"aux": buddy[level]})

    def products(_, piece):
        k, c = piece
        mine = near(n, k)
        cols, _, w = span(piece)
        m = len(mine) * VB
        if c == 0:
            for s, offset in enumerate(mine):
                if not (n == 4 and offset == 2):
                    arrivals[offset].wait_recv()
                hi, low = split(srecv[offs.index(offset)])
                ahi[s * VB:(s + 1) * VB, :] = hi
                ahi[m + s * VB:m + (s + 1) * VB, :] = low
        t = dot_t(ahi[:2 * m, :], bhi[cols, :])
        u = dot_t(ahi[:m, :], blo[cols, :])
        cur[k][0][:, :, cols] = (t[:m] + t[m:] + u).reshape(len(mine), VB, w)
        start_level(0, piece)

    def reduce_level(level, piece):
        k, c = piece
        cols, dcols, _ = span(piece)
        half = VB >> (level + 1)
        flying["reduce", level, piece].wait_recv()
        keep = pl.multiple_of(bits[level] * half, 8)
        cur[k][level + 1][:, :, cols] = cur[k][level][:, pl.ds(keep, half), cols] + rec[k][level][:, :, cols]
        if level + 1 < levels:
            start_level(level + 1, piece)
        else:
            flying["ex", piece] = push(
                cur[k][levels].at[near(n, k).index(n - k), :, dcols],
                ex.at[k - 1, :, dcols], {"occ": occ_at(n - k)})

    def amplitudes(_, piece):
        k, c = piece
        cols, _, w = span(piece)
        if c == 0:
            e_copies[2 - k].wait_recv()
        flying["ex", piece].wait_recv()
        coul = cur[k][levels][near(n, k).index(k), :, cols]
        exch = ex[k - 1, :, cols]
        base = evc[pl.ds(lo, rows), 0:1] - eocc[k - 1, 0:1, 0:1] - esend[0:1, 0:1]
        val = (2.0 * coul - exch) / (base + evp[:, cols])
        prod = coul * val
        part = eacc[k - 1]
        for t in range(w // 128):
            part = part + prod[:, t * 128:(t + 1) * 128]
        eacc[k - 1] = part
        if c == parts[k] - 1:
            column = lax.broadcasted_iota(jnp.int32, (rows, w), 1) + c * w
            val = jnp.where(column < nv, val, jnp.sum(part, axis=1, keepdims=True))
        amp[k - 1, pl.ds(lo, rows), cols] = val
        start_gather(levels - 1, piece)

    def gather_level(level, piece):
        flying["gather", level, piece].wait_recv()
        start_gather(level - 1, piece)

    final = []

    def gammas(_, piece):
        k, c = piece
        cols, _, w = span(piece)
        last = c == parts[k] - 1
        flying["gather", 0, piece].wait_recv()
        if last:
            total = jnp.sum(amp[k - 1, :, width - 128:], axis=0, keepdims=True)
            psend[k - 1] = jnp.broadcast_to(total[:, 127:128], (8, 128))
            final.append(push(psend.at[k - 1], precv.at[k - 1], {"occ": occ_at(k)}))
        hi, low = split(amp[k - 1, :, cols])
        t = dot(jnp.concatenate([hi, low], axis=0), bhi[cols, :])
        part = t[:VB] + t[VB:] + dot(hi, blo[cols, :])
        gsend[k - 1] = part if c == 0 else gsend[k - 1] + part
        if last:
            final.append(push(gsend.at[k - 1], grecv.at[k - 1], {"occ": occ_at(k)}))

    run = {"products": products, "reduce": reduce_level, "amplitudes": amplitudes,
           "gather": gather_level, "gammas": gammas}
    for stage, level, piece in schedule(levels, parts):
        run[stage](level, piece)

    for copy in final:
        copy.wait_recv()
    lane = lax.broadcasted_iota(jnp.int32, (8, 128), 1)
    eout[...] = jnp.where(lane == 0, precv[0], precv[1])[0:1, 0:2]
    gout[...] = grecv[0] + grecv[1]
    for copy, when in sends:
        if when is None:
            copy.wait_send()
        else:
            pl.when(when)(copy.wait_send)


def body(n, m, b_tensor, eps_occ, eps_virt):
    _, depth, nv = b_tensor.shape
    width = (nv // 128 + 1) * 128
    levels = m.bit_length() - 1
    offs = set(near(n, 1) + near(n, 2))
    ne = len(offs)
    tiles = width // 128
    parts = {k: p if tiles % p == 0 else 1 for k, p in PARTS.items()}
    rows = VB >> levels
    scratch = [
        pltpu.VMEM((width, depth), F32),
        pltpu.VMEM((width, depth), BF16),
        pltpu.VMEM((width, depth), BF16),
        pltpu.VMEM((ne, VB, depth), F32),
        pltpu.VMEM((4 * VB, depth), BF16),
        pltpu.VMEM((1, width), F32),
        pltpu.VMEM((128, 128), F32),
        pltpu.VMEM((8, 128), F32),
        pltpu.VMEM((2, 8, 128), F32),
        pltpu.VMEM((2, VB, width), F32),
        pltpu.VMEM((2, rows, width), F32),
        pltpu.VMEM((2, rows, 128), F32),
        pltpu.VMEM((2, VB, depth), F32),
        pltpu.VMEM((2, VB, depth), F32),
        pltpu.VMEM((2, 8, 128), F32),
        pltpu.VMEM((2, 8, 128), F32),
    ]
    for k in (1, 2):
        blocks = len(near(n, k))
        scratch += [pltpu.VMEM((blocks, VB >> level, width), F32) for level in range(levels + 1)]
        scratch += [pltpu.VMEM((blocks, VB >> (level + 1), width), F32) for level in range(levels)]
    copies = ne + 8 + (parts[1] + parts[2]) * (2 * levels + 1)
    scratch += [
        pltpu.SemaphoreType.DMA((1,)),
        pltpu.SemaphoreType.DMA((copies,)),
        pltpu.SemaphoreType.DMA((ne + copies,)),
    ]
    flops = 6 * depth * width * VB * (ne + 2)
    gamma, energy = pl.pallas_call(
        functools.partial(kernel, n, levels, parts, nv),
        out_shape=(jax.ShapeDtypeStruct((VB, depth), F32), jax.ShapeDtypeStruct((1, 2), F32)),
        in_specs=[
            pl.BlockSpec(memory_space=pl.ANY),
            pl.BlockSpec(memory_space=pltpu.SMEM),
            pl.BlockSpec(memory_space=pltpu.VMEM),
        ],
        out_specs=(pl.BlockSpec(memory_space=pltpu.VMEM), pl.BlockSpec(memory_space=pltpu.VMEM)),
        scratch_shapes=scratch,
        compiler_params=pltpu.CompilerParams(
            collective_id=0, has_side_effects=True, vmem_limit_bytes=VMEM_MIB * 2 ** 20),
        cost_estimate=pl.CostEstimate(flops=flops, bytes_accessed=4 * depth * nv, transcendentals=0),
    )(jnp.swapaxes(b_tensor, 1, 2), eps_occ, eps_virt.reshape(1, nv))
    return gamma.T[None], energy


def solution(mesh):
    placed = (P(("groups", "occ"), "aux", None), P(("groups", "occ")), P("groups"))
    return jax.shard_map(
        functools.partial(body, mesh.shape["occ"], mesh.shape["aux"]),
        mesh=mesh,
        in_specs=placed,
        out_specs=(P(("groups", "occ"), "aux", None), P(("groups", "occ"), None)),
        check_vma=False,
    )
```

time: 68.1 us -> 59.1 us (0.87); the launches traced: 67.9 us -> 58 us
  local copies, waits for them, and re-layouts: 10.1 us -> 4.02 us
  Pallas kernels: 56.5 us -> 52.7 us
    unnamed x5 -> x2, local copies, waits for them, and re-layouts: 9.39 us -> 2.73 us
    pallas_call x1, Pallas kernels: 56.5 us -> 52.7 us  [body(): pl.pallas_call(functools.partial(kernel, n, levels, parts, nv), out_shape...]
where the time goes in v2:
time: 59.1 us; the launch traced here: 58 us
  Pallas kernels  52.7 us (89%)
  local copies, waits for them, and re-layouts  4.02 us (7%)
  between operations  1.29 us (2%)
    pallas_call x1, Pallas kernels, body(): pl.pallas_call(functools.partial(kernel, n, levels, parts, nv), out_shape...  52.7 us
    unnamed x2, local copies, waits for them, and re-layouts  2.73 us
    reshape x1, local copies, waits for them, and re-layouts, body(): eps_virt.reshape(1, nv)  1.3 us

profile of v2, /device:TPU:0, one launch (start us, length us, event | category | flops | bytes accessed | tf_op | source)
XLA Modules:
  0.0 58.0 jit_solution(11727294465534944942)
XLA Ops:
  1.3 1.3 %reshape.7.refs_2_ = f32[1,1800]{1,0:T(1,128)} reshape(f32[1800]{0:T(1024)} %param.5) | data formatting | bytes 14400 | tf_op jit(solution)/shard_map/reshape | solution.py:313
  2.6 52.7 %shard_map.50 = (f32[64,640]{1,0:T(8,128)}, f32[1,2]{1,0:T(1,128)}) custom-call(f32[1,1800,640]{2,1,0:T(8,128)} %bitcast.5, f32[1]{0:T(128)S(6)} %copy.7.refs_1_, f32[1,1800]{1,0:T(1,128)} %reshape.7.refs_2_), custom_call_target="tpu_custom_call" | custom-call | flops 2359296000 | bytes 4608000 | tf_op jit(solution)/shard_map/pallas_call | solution.py:300
  55.3 1.6 %copy.8 = f32[1,640,64]{1,2,0:T(8,128)} copy(f32[1,640,64]{1,2,0:T(8,128)} %bitcast.4) | data formatting | bytes 327680
  56.8 1.1 %copy.9 = f32[1,2]{1,0:T(1,128)} copy(f32[1,2]{1,0:T(1,128)} %get-tuple-element.9) | data formatting | bytes 16

commit v3 on v2

v3 whole, which is shorter than its diff:
```python
import functools

import jax
import jax.numpy as jnp
from jax import lax
from jax.experimental import pallas as pl
from jax.experimental.pallas import tpu as pltpu
from jax.sharding import PartitionSpec as P

VB = 64
HALVES = 2
VMEM_MIB = 60
MESH = pl.DeviceIdType.MESH
F32 = jnp.float32
BF16 = jnp.bfloat16


def split(x):
    hi = x.astype(BF16)
    return hi, (x - hi.astype(F32)).astype(BF16)


def dot(x, y):
    return lax.dot_general(x, y, (((1,), (0,)), ((), ())), preferred_element_type=F32)


def dot_t(x, y):
    return lax.dot_general(x, y, (((1,), (1,)), ((), ())), preferred_element_type=F32)


def near(n, k):
    return sorted({k % n, (n - k) % n})


def schedule(levels, halves):
    pieces = [(k, h) for h in range(halves) for k in (2, 1)]
    stages = [("products", 0)] + [("reduce", level) for level in range(levels)] + [("amplitudes", 0)]
    stages += [("gather", level) for level in range(levels - 1, 0, -1)] + [("gammas", 0)]
    order = []
    for t in range(len(pieces) + len(stages) - 1):
        for s in reversed(range(len(stages))):
            if 0 <= t - s < len(pieces):
                order.append((*stages[s], pieces[t - s]))
    return order


def kernel(n, levels, halves, nv, *refs):
    b_hbm, eo_ref, ev_ref, gout, eout = refs[:5]
    (bv, bhi, blo, srecv, ahi, evp, evc, esend, eocc, amp, ex,
     gsend, grecv, psend, precv) = refs[5:20]
    at = 20
    cur, rec = {}, {}
    for k in (1, 2):
        cur[k] = refs[at:at + levels + 1]
        rec[k] = refs[at + levels + 1:at + 2 * levels + 1]
        at += 2 * levels + 1
    load_sem, send_sem, recv_sem = refs[at:]

    offs = sorted(set(near(n, 1) + near(n, 2)))
    ne = len(offs)
    width, depth = bhi.shape
    me = lax.axis_index("occ")
    aux = lax.axis_index("aux")
    bits = [lax.rem(lax.div(aux, 2 ** level), 2) for level in range(levels)]
    buddy = [aux + (1 - 2 * bits[level]) * 2 ** level for level in range(levels)]
    part = VB // halves
    rows = part >> levels

    starts = []
    lo = 0
    for level in range(levels):
        lo = lo + bits[level] * (part >> (level + 1))
        starts.append(pl.multiple_of(lo, 8))
    lo = starts[-1]

    sends = []

    def occ_at(offset):
        return lax.rem(me + offset, n)

    def push(src, dst, target, slot=None, when=None):
        k = len(sends)
        copy = pltpu.make_async_remote_copy(
            src_ref=src, dst_ref=dst, send_sem=send_sem.at[k],
            recv_sem=recv_sem.at[ne * halves + k if slot is None else slot],
            device_id=target, device_id_type=MESH)
        if when is None:
            copy.start()
        else:
            pl.when(when)(copy.start)
        sends.append((copy, when))
        return copy

    barrier = pltpu.get_barrier_semaphore()
    for offset in offs:
        pl.semaphore_signal(barrier, inc=1, device_id={"occ": occ_at(offset)}, device_id_type=MESH)
    for level in range(levels):
        pl.semaphore_signal(barrier, inc=1, device_id={"aux": buddy[level]}, device_id_type=MESH)
    load = pltpu.make_async_copy(b_hbm.at[0], bv.at[pl.ds(0, nv), :], load_sem.at[0])
    load.start()
    esend[...] = jnp.full((8, 128), eo_ref[0], F32)
    pl.semaphore_wait(barrier, ne + levels)

    arrivals = {}

    def share(offset, h, when=None):
        slot = offs.index(offset)
        block = pl.ds(h * part, part)
        arrivals[offset, h] = push(
            b_hbm.at[0, block, :], srecv.at[slot, block, :], {"occ": occ_at(n - offset)},
            slot * halves + h, when)

    def share_all(h):
        for offset in near(n, 2):
            share(offset, h)
        if n == 4:
            share(1, h, me > 0)
            share(3, h, me < 3)
        else:
            for offset in near(n, 1):
                share(offset, h)

    def pass_on(h):
        if n == 4:
            arrivals[2, h].wait_recv()
            block = pl.ds(h * part, part)
            for offset, middle in ((1, 2), (3, 1)):
                slot = offs.index(offset)
                push(srecv.at[offs.index(2), block, :], srecv.at[slot, block, :],
                     {"occ": occ_at(offset)}, slot * halves + h, me == middle)

    share_all(0)
    e_copies = [push(esend, eocc.at[k - 1], {"occ": occ_at(n - k)}) for k in (2, 1)]

    evp[...] = jnp.ones_like(evp)
    evp[:, :nv] = ev_ref[...]
    evc[...] = jnp.broadcast_to(evp[:, :128], (128, 128)).T
    bv[nv:, :] = jnp.zeros((width - nv, depth), F32)
    load.wait()

    @pl.loop(0, width // 16)
    def _(t):
        block = pl.ds(pl.multiple_of(t * 16, 16), 16)
        hi, low = split(bv[block, :])
        bhi[block, :] = hi
        blo[block, :] = low

    pass_on(0)
    for h in range(1, halves):
        share_all(h)

    flying = {}

    def start_level(level, piece):
        k, h = piece
        half = part >> (level + 1)
        away = pl.multiple_of((1 - bits[level]) * half, 8)
        flying["reduce", level, piece] = push(
            cur[k][level].at[h, :, pl.ds(away, half), :], rec[k][level].at[h],
            {"aux": buddy[level]})

    def start_gather(level, piece):
        k, h = piece
        block = amp.at[k - 1, h, pl.ds(starts[level], part >> (level + 1)), :]
        flying["gather", level, piece] = push(block, block, {"aux": buddy[level]})

    def products(_, piece):
        k, h = piece
        mine = near(n, k)
        m = len(mine) * part
        if k == 2 and h > 0:
            pass_on(h)
        for s, offset in enumerate(mine):
            if not (n == 4 and offset == 2):
                arrivals[offset, h].wait_recv()
            hi, low = split(srecv[offs.index(offset), h * part:(h + 1) * part, :])
            ahi[s * part:(s + 1) * part, :] = hi
            ahi[m + s * part:m + (s + 1) * part, :] = low
        t = dot_t(ahi[:2 * m, :], bhi[...])
        u = dot_t(ahi[:m, :], blo[...])
        cur[k][0][h] = (t[:m] + t[m:] + u).reshape(len(mine), part, width)
        start_level(0, piece)

    def reduce_level(level, piece):
        k, h = piece
        half = part >> (level + 1)
        flying["reduce", level, piece].wait_recv()
        keep = pl.multiple_of(bits[level] * half, 8)
        cur[k][level + 1][h] = cur[k][level][h, :, pl.ds(keep, half), :] + rec[k][level][h]
        if level + 1 < levels:
            start_level(level + 1, piece)
        else:
            flying["ex", piece] = push(
                cur[k][levels].at[h, near(n, k).index(n - k)], ex.at[k - 1, h],
                {"occ": occ_at(n - k)})

    def amplitudes(_, piece):
        k, h = piece
        if h == 0:
            e_copies[2 - k].wait_recv()
        flying["ex", piece].wait_recv()
        coul = cur[k][levels][h, near(n, k).index(k)]
        exch = ex[k - 1, h]
        row = pl.multiple_of(h * part + lo, 8)
        base = evc[pl.ds(row, rows), 0:1] - eocc[k - 1, 0:1, 0:1] - esend[0:1, 0:1]
        val = (2.0 * coul - exch) / (base + evp[...])
        energy = jnp.sum(coul * val, axis=1, keepdims=True)
        column = lax.broadcasted_iota(jnp.int32, (rows, width), 1)
        amp[k - 1, h, pl.ds(lo, rows), :] = jnp.where(column < nv, val, energy)
        start_gather(levels - 1, piece)

    def gather_level(level, piece):
        flying["gather", level, piece].wait_recv()
        start_gather(level - 1, piece)

    final = []

    def gammas(_, piece):
        k, h = piece
        flying["gather", 0, piece].wait_recv()
        hi, low = split(amp[k - 1, h])
        t = dot(jnp.concatenate([hi, low], axis=0), bhi[...])
        gsend[k - 1, h] = t[:part] + t[part:] + dot(hi, blo[...])
        final.append(push(gsend.at[k - 1, h], grecv.at[k - 1, h], {"occ": occ_at(k)}))
        if h == halves - 1:
            ends = amp[k - 1, :, :, width - 128:].reshape(VB, 128)
            total = jnp.sum(ends, axis=0, keepdims=True)
            psend[k - 1] = jnp.broadcast_to(total[:, 127:128], (8, 128))
            final.append(push(psend.at[k - 1], precv.at[k - 1], {"occ": occ_at(k)}))

    run = {"products": products, "reduce": reduce_level, "amplitudes": amplitudes,
           "gather": gather_level, "gammas": gammas}
    for stage, level, piece in schedule(levels, halves):
        run[stage](level, piece)

    for copy in final:
        copy.wait_recv()
    lane = lax.broadcasted_iota(jnp.int32, (8, 128), 1)
    eout[...] = jnp.where(lane == 0, precv[0], precv[1])[0:1, 0:2]
    gout[...] = (grecv[0] + grecv[1]).reshape(VB, depth)
    for copy, when in sends:
        if when is None:
            copy.wait_send()
        else:
            pl.when(when)(copy.wait_send)


def body(n, m, b_tensor, eps_occ, eps_virt):
    _, depth, nv = b_tensor.shape
    width = (nv // 128 + 1) * 128
    levels = m.bit_length() - 1
    offs = set(near(n, 1) + near(n, 2))
    ne = len(offs)
    halves = HALVES if VB % (8 * HALVES * m) == 0 else 1
    part = VB // halves
    rows = part >> levels
    scratch = [
        pltpu.VMEM((width, depth), F32),
        pltpu.VMEM((width, depth), BF16),
        pltpu.VMEM((width, depth), BF16),
        pltpu.VMEM((ne, VB, depth), F32),
        pltpu.VMEM((4 * VB, depth), BF16),
        pltpu.VMEM((1, width), F32),
        pltpu.VMEM((128, 128), F32),
        pltpu.VMEM((8, 128), F32),
        pltpu.VMEM((2, 8, 128), F32),
        pltpu.VMEM((2, halves, part, width), F32),
        pltpu.VMEM((2, halves, rows, width), F32),
        pltpu.VMEM((2, halves, part, depth), F32),
        pltpu.VMEM((2, halves, part, depth), F32),
        pltpu.VMEM((2, 8, 128), F32),
        pltpu.VMEM((2, 8, 128), F32),
    ]
    for k in (1, 2):
        blocks = len(near(n, k))
        scratch += [pltpu.VMEM((halves, blocks, part >> level, width), F32) for level in range(levels + 1)]
        scratch += [pltpu.VMEM((halves, blocks, part >> (level + 1), width), F32) for level in range(levels)]
    copies = (ne + 4) * halves + 4 + 2 * halves * (2 * levels + 1)
    scratch += [
        pltpu.SemaphoreType.DMA((1,)),
        pltpu.SemaphoreType.DMA((copies,)),
        pltpu.SemaphoreType.DMA((ne * halves + copies,)),
    ]
    flops = 6 * depth * width * VB * (ne + 2)
    gamma, energy = pl.pallas_call(
        functools.partial(kernel, n, levels, halves, nv),
        out_shape=(jax.ShapeDtypeStruct((VB, depth), F32), jax.ShapeDtypeStruct((1, 2), F32)),
        in_specs=[
            pl.BlockSpec(memory_space=pl.ANY),
            pl.BlockSpec(memory_space=pltpu.SMEM),
            pl.BlockSpec(memory_space=pltpu.VMEM),
        ],
        out_specs=(pl.BlockSpec(memory_space=pltpu.VMEM), pl.BlockSpec(memory_space=pltpu.VMEM)),
        scratch_shapes=scratch,
        compiler_params=pltpu.CompilerParams(
            collective_id=0, has_side_effects=True, vmem_limit_bytes=VMEM_MIB * 2 ** 20),
        cost_estimate=pl.CostEstimate(flops=flops, bytes_accessed=4 * depth * nv, transcendentals=0),
    )(jnp.swapaxes(b_tensor, 1, 2), eps_occ, eps_virt.reshape(1, nv))
    return gamma.T[None], energy


def solution(mesh):
    placed = (P(("groups", "occ"), "aux", None), P(("groups", "occ")), P("groups"))
    return jax.shard_map(
        functools.partial(body, mesh.shape["occ"], mesh.shape["aux"]),
        mesh=mesh,
        in_specs=placed,
        out_specs=(P(("groups", "occ"), "aux", None), P(("groups", "occ"), None)),
        check_vma=False,
    )
```

time: 59.1 us -> 52.5 us (0.89); the launches traced: 58 us -> 52.2 us
  Pallas kernels: 52.7 us -> 46.9 us
    pallas_call x1, Pallas kernels: 52.7 us -> 46.9 us  [body(): pl.pallas_call(functools.partial(kernel, n, levels, halves, nv), out_shap...]
where the time goes in v3:
time: 52.5 us; the launch traced here: 52.2 us
  Pallas kernels  46.9 us (89%)
  local copies, waits for them, and re-layouts  4.02 us (8%)
  between operations  1.29 us (2%)
    pallas_call x1, Pallas kernels, body(): pl.pallas_call(functools.partial(kernel, n, levels, halves, nv), out_shap...  46.9 us
    unnamed x2, local copies, waits for them, and re-layouts  2.73 us
    reshape x1, local copies, waits for them, and re-layouts, body(): eps_virt.reshape(1, nv)  1.3 us

profile of v3, /device:TPU:0, one launch (start us, length us, event | category | flops | bytes accessed | tf_op | source)
XLA Modules:
  0.0 52.2 jit_solution(1261006259556816246)
XLA Ops:
  1.3 1.3 %reshape.7.refs_2_ = f32[1,1800]{1,0:T(1,128)} reshape(f32[1800]{0:T(1024)} %param.5) | data formatting | bytes 14400 | tf_op jit(solution)/shard_map/reshape | solution.py:298
  2.6 46.9 %shard_map.50 = (f32[64,640]{1,0:T(8,128)}, f32[1,2]{1,0:T(1,128)}) custom-call(f32[1,1800,640]{2,1,0:T(8,128)} %bitcast.5, f32[1]{0:T(128)S(6)} %copy.7.refs_1_, f32[1,1800]{1,0:T(1,128)} %reshape.7.refs_2_), custom_call_target="tpu_custom_call" | custom-call | flops 2359296000 | bytes 4608000 | tf_op jit(solution)/shard_map/pallas_call | solution.py:285
  49.5 1.6 %copy.8 = f32[1,640,64]{1,2,0:T(8,128)} copy(f32[1,640,64]{1,2,0:T(8,128)} %bitcast.4) | data formatting | bytes 327680
  51.1 1.1 %copy.9 = f32[1,2]{1,0:T(1,128)} copy(f32[1,2]{1,0:T(1,128)} %get-tuple-element.9) | data formatting | bytes 16

commit v4 on v3

--- a/solution.py
+++ b/solution.py
@@ -9,7 +9,7 @@
 
 VB = 64
 HALVES = 2
-VMEM_MIB = 60
+VMEM_MIB = 52
 MESH = pl.DeviceIdType.MESH
 F32 = jnp.float32
 BF16 = jnp.bfloat16

time: 52.5 us -> 49 us (0.933)
  local copies, waits for them, and re-layouts: 4.02 us -> 1.88 us
  Pallas kernels: 46.9 us -> 45.6 us
    unnamed x2, local copies, waits for them, and re-layouts: 2.73 us -> 1.18 us
    pallas_call x1, Pallas kernels: 46.9 us -> 45.6 us  [body(): pl.pallas_call(functools.partial(kernel, n, levels, halves, nv), out_shap...]
    reshape x1, local copies, waits for them, and re-layouts: 1.3 us -> 0.7 us  [body(): eps_virt.reshape(1, nv)]
where the time goes in v4:
time: 49 us; the launch traced here: 48.7 us
  Pallas kernels  45.6 us (93%)
  local copies, waits for them, and re-layouts  1.88 us (4%)
  between operations  1.29 us (3%)
    pallas_call x1, Pallas kernels, body(): pl.pallas_call(functools.partial(kernel, n, levels, halves, nv), out_shap...  45.6 us
    unnamed x2, local copies, waits for them, and re-layouts  1.18 us

profile of v4, /device:TPU:0, one launch (start us, length us, event | category | flops | bytes accessed | tf_op | source)
XLA Modules:
  0.0 48.7 jit_solution(10788648978066751015)
XLA Ops:
  1.3 0.7 %reshape.7.refs_2_ = f32[1,1800]{1,0:T(1,128)S(1)} reshape(f32[1800]{0:T(1024)} %param.5) | data formatting | bytes 14400 | tf_op jit(solution)/shard_map/reshape | solution.py:298
  2.0 45.6 %shard_map.50 = (f32[64,640]{1,0:T(8,128)S(1)}, f32[1,2]{1,0:T(1,128)S(1)}) custom-call(f32[1,1800,640]{2,1,0:T(8,128)} %bitcast.5, f32[1]{0:T(128)S(6)} %copy.7.refs_1_, f32[1,1800]{1,0:T(1,128)S(1)} %reshape.7.refs_2_), custom_call_target="tpu_custom_call" | custom-call | flops 2359296000 | bytes 4608000 | tf_op jit(solution)/shard_map/pallas_call | solution.py:285
  47.5 0.7 %copy.8 = f32[1,640,64]{1,2,0:T(8,128)} copy(f32[1,640,64]{1,2,0:T(8,128)S(1)} %bitcast.4) | data formatting | bytes 327680
  48.2 0.5 %copy.9 = f32[1,2]{1,0:T(1,128)} copy(f32[1,2]{1,0:T(1,128)S(1)} %get-tuple-element.9) | data formatting | bytes 16

commit v5 on v4

--- a/solution.py
+++ b/solution.py
@@ -214,14 +214,21 @@
         start_gather(level - 1, piece)
 
     final = []
+    between = {}
 
     def gammas(_, piece):
         k, h = piece
         flying["gather", 0, piece].wait_recv()
         hi, low = split(amp[k - 1, h])
         t = dot(jnp.concatenate([hi, low], axis=0), bhi[...])
-        gsend[k - 1, h] = t[:part] + t[part:] + dot(hi, blo[...])
-        final.append(push(gsend.at[k - 1, h], grecv.at[k - 1, h], {"occ": occ_at(k)}))
+        value = t[:part] + t[part:] + dot(hi, blo[...])
+        if k == 2:
+            gsend[1, h] = value
+            between[h] = push(gsend.at[1, h], grecv.at[1, h], {"occ": occ_at(1)})
+        else:
+            between[h].wait_recv()
+            gsend[0, h] = value + grecv[1, h]
+            final.append(push(gsend.at[0, h], grecv.at[0, h], {"occ": occ_at(1)}))
         if h == halves - 1:
             ends = amp[k - 1, :, :, width - 128:].reshape(VB, 128)
             total = jnp.sum(ends, axis=0, keepdims=True)
@@ -237,7 +244,7 @@
         copy.wait_recv()
     lane = lax.broadcasted_iota(jnp.int32, (8, 128), 1)
     eout[...] = jnp.where(lane == 0, precv[0], precv[1])[0:1, 0:2]
-    gout[...] = (grecv[0] + grecv[1]).reshape(VB, depth)
+    gout[...] = grecv[0].reshape(VB, depth)
     for copy, when in sends:
         if when is None:
             copy.wait_send()

time: 49 us -> 49.1 us (level)
  no operation moved by 1% of the time
where the time goes in v5:
time: 49.1 us; the launch traced here: 48.9 us
  Pallas kernels  45.7 us (93%)
  local copies, waits for them, and re-layouts  1.88 us (4%)
  between operations  1.29 us (3%)
    pallas_call x1, Pallas kernels, body(): pl.pallas_call(functools.partial(kernel, n, levels, halves, nv), out_shap...  45.7 us
    unnamed x2, local copies, waits for them, and re-layouts  1.18 us

profile of v5, /device:TPU:0, one launch (start us, length us, event | category | flops | bytes accessed | tf_op | source)
XLA Modules:
  0.0 48.9 jit_solution(15252161165889962725)
XLA Ops:
  1.3 0.7 %reshape.7.refs_2_ = f32[1,1800]{1,0:T(1,128)S(1)} reshape(f32[1800]{0:T(1024)} %param.5) | data formatting | bytes 14400 | tf_op jit(solution)/shard_map/reshape | solution.py:305
  2.0 45.7 %shard_map.50 = (f32[64,640]{1,0:T(8,128)S(1)}, f32[1,2]{1,0:T(1,128)S(1)}) custom-call(f32[1,1800,640]{2,1,0:T(8,128)} %bitcast.5, f32[1]{0:T(128)S(6)} %copy.7.refs_1_, f32[1,1800]{1,0:T(1,128)S(1)} %reshape.7.refs_2_), custom_call_target="tpu_custom_call" | custom-call | flops 2359296000 | bytes 4608000 | tf_op jit(solution)/shard_map/pallas_call | solution.py:292
  47.7 0.7 %copy.8 = f32[1,640,64]{1,2,0:T(8,128)} copy(f32[1,640,64]{1,2,0:T(8,128)S(1)} %bitcast.4) | data formatting | bytes 327680
  48.4 0.5 %copy.9 = f32[1,2]{1,0:T(1,128)} copy(f32[1,2]{1,0:T(1,128)S(1)} %get-tuple-element.9) | data formatting | bytes 16
